TPU v7x, 32 devices: a whole 2x2x4 slice. The times are simulated.
32 devices in a mesh: span: 16 (over z, y, x), width: 2 (over core).
Axes of the slice: x: 2, y: 2, z: 4, core: 2. Of those that a mesh axis runs over, the one named last changes fastest.
Arguments:
- state: float32 [4, 128, 64, 128], P(None, 'span', 'width'), may hold values from 0.2 to 2
- source: float32 [4, 128, 64, 128], P(None, 'span', 'width'), may hold values from -6 to 8
- conductance: float32 [128, 64, 128], P('span', 'width'), may hold values from 0.5 to 2
- rebar_cover: int32 [128, 64, 128], P('span', 'width'), may hold values 0 or 1
- colour: int32 [16, 2], P('span', 'width'), may hold values from 0 to 1
- diffusivity: float32 [4], replicated, may hold values from 0.5 to 2
- binding: float32 [4], replicated, may hold values from 0.1 to 1
Outputs:
- updated: float32 [4, 128, 64, 128], P(None, 'span', 'width')
- residual: float32 [4, 128, 64, 128], P(None, 'span', 'width')
All inputs are finite; a program needn't handle non-finite values. No bound on the sum of `rebar_cover` on one device may be relied on, other than what follows from the above.
Results may differ from a plain program's by a relative error of at most 0.002.
Values sent between devices are 32-bit elements; how exact they have to be, the bound alone decides.
A program may use at most 64 MiB of HBM per device.

v0:
```python
import jax
import jax.numpy as jnp
from jax import lax
from jax.sharding import PartitionSpec as P

COARSEN = 8
SWEEPS = 4
COARSE_ITERS = 20


INV_STEP = 0.05
EPSILON = 1e-06


def padded(shard, sides, width):
    for axis, dim in sides:
        size, length = (lax.axis_size(axis), shard.shape[dim])
        up = [(i, (i + 1) % size) for i in range(size - 1)]
        down = [(j, i) for i, j in up]
        last = lax.slice_in_dim(shard, length - width, length, axis=dim)
        first = lax.slice_in_dim(shard, 0, width, axis=dim)
        before = lax.ppermute(last, axis, up)
        after = lax.ppermute(first, axis, down)
        shard = jnp.concatenate([before, shard, after], axis=dim)
    return shard


def field_rim(field):
    return padded(field, (("span", 1), ("width", 2)), 1)


def later_z(value):
    return jnp.pad(value[..., 1:], ((0, 0), (0, 0), (0, 0), (0, 1)))


def earlier_z(value):
    return jnp.pad(value[..., :-1], ((0, 0), (0, 0), (0, 0), (1, 0)))


def padded_sum(full):
    inner = full[:, 1:-1, 1:-1, :]
    total = full[:, 2:, 1:-1, :] + full[:, :-2, 1:-1, :]
    total = total + full[:, 1:-1, 2:, :]
    total = total + full[:, 1:-1, :-2, :]
    total = total + later_z(inner)
    total = total + earlier_z(inner)
    return total


def block_sum(value):
    lead, n_one, n_two, n_three = value.shape
    shaped = value.reshape(
        lead, n_one // COARSEN, COARSEN, n_two // COARSEN, COARSEN, n_three // COARSEN, COARSEN
    )
    return shaped.sum(axis=(2, 4, 6))


def on_device(state, source, conductance, rebar_cover, colour, diffusivity, binding):
    ions, cx, cy, cz = state.shape
    spread = diffusivity[:, None, None, None]
    strength = binding[:, None, None, None]
    cover = rebar_cover.astype(jnp.float32)[None]
    coef = spread * conductance[None]
    bound_term = cover * strength * state / (1.0 + state)
    mass = INV_STEP + cover * strength / ((1.0 + state) * (1.0 + state))
    diag = mass + 6.0 * coef
    rhs = source - (coef * (6.0 * state - padded_sum(field_rim(state))) + bound_term)
    start_x = lax.axis_index("span") * cx
    start_y = lax.axis_index("width") * cy
    glob_x = start_x + jnp.arange(cx, dtype=jnp.int32)
    glob_y = start_y + jnp.arange(cy, dtype=jnp.int32)
    glob_z = jnp.arange(cz, dtype=jnp.int32)
    parity = (glob_x[:, None, None] + glob_y[None, :, None] + glob_z[None, None, :]) % 2
    mine = colour[0, 0]
    delta = jnp.zeros_like(state)
    for phase in range(2):
        if phase == 0:
            frozen = jnp.zeros((ions, cx + 2, cy + 2, cz), jnp.float32)
        else:
            frozen = field_rim(delta)
        active = mine == phase
        for sweep in range(SWEEPS):
            for side in range(2):
                full = frozen.at[:, 1:-1, 1:-1, :].set(delta)
                total = padded_sum(full)
                fresh = (rhs + coef * total) / diag
                chosen = jnp.logical_and(active, parity == side)[None]
                delta = jnp.where(chosen, fresh, delta)
    fine = rhs - (diag * delta - coef * padded_sum(field_rim(delta)))
    coarse_rhs = block_sum(fine)
    cond_sum = block_sum(conductance[None])
    coarse_off = spread * cond_sum / COARSEN
    coarse_diag = block_sum(mass) + 6.0 * coarse_off

    def jacobi_local(step, value):
        outer = padded(value, (("span", 1), ("width", 2)), 1)
        return (coarse_rhs + coarse_off * padded_sum(outer)) / coarse_diag

    coarse = lax.fori_loop(0, COARSE_ITERS, jacobi_local, jnp.zeros_like(coarse_rhs))
    lift = jnp.repeat(
        jnp.repeat(jnp.repeat(coarse, COARSEN, axis=1), COARSEN, axis=2), COARSEN, axis=3
    )
    lift_full = field_rim(lift)
    image = diag * lift - coef * padded_sum(lift_full)
    numer, denom = lax.psum(
        (jnp.sum(fine * image, axis=(1, 2, 3)), jnp.sum(image * image, axis=(1, 2, 3))),
        ("span", "width"),
    )
    weight = (numer / (denom + EPSILON))[:, None, None, None]
    delta = delta + weight * lift
    outer_delta = padded(delta, (("span", 1), ("width", 2)), 1)
    final = rhs - (diag * delta - coef * padded_sum(outer_delta))
    return (state + delta, final)


def solution(mesh):
    in_specs = (
        P(None, "span", "width", None),
        P(None, "span", "width", None),
        P("span", "width", None),
        P("span", "width", None),
        P("span", "width"),
        P(),
        P(),
    )
    out_specs = (P(None, "span", "width", None), P(None, "span", "width", None))
    return jax.shard_map(
        on_device, mesh=mesh, in_specs=in_specs, out_specs=out_specs, check_vma=False
    )
```

profile of v0, /device:TPU:0, one launch (start us, length us, event | category | flops | bytes accessed | tf_op | source)
XLA Modules:
  0.0 468.2 jit_solution(14834427199915836394)
XLA Ops:
  2.8 5.5 %collective-permute-start.5 = (f32[4,1,32,128]{3,2,1,0:T(8,128)S(1)}, f32[4,1,32,128]{3,2,1,0:T(8,128)S(1)}, u32[]{:S(2)}, u32[]{:S(2)}) collective-permute-start(f32[4,1,32,128]{3,2,1,0:T(8,128)S(1)} %get-tuple-element.365), channel_id=1, source_target_pairs={{0,2},{2,4},{4,6},{6,8},{8,10},{10,12},{12,14},{14,16},{16,18},{18... | collective-permute-start | bytes 196616 | tf_op jit(solution)/shard_map/ppermute | solution.py:22
  23.3 4.8 %collective-permute-start.8 = (f32[4,1,32,128]{3,2,1,0:T(8,128)}, f32[4,1,32,128]{3,2,1,0:T(8,128)S(1)}, u32[]{:S(2)}, u32[]{:S(2)}) collective-permute-start(f32[4,1,32,128]{3,2,1,0:T(8,128)} %get-tuple-element.348), channel_id=1, source_target_pairs={{0,2},{2,4},{4,6},{6,8},{8,10},{10,12},{12,14},{14,16},{16,18},{18... | collective-permute-start | bytes 196616 | tf_op jit(solution)/shard_map/ppermute | solution.py:22
  86.9 4.7 %collective-permute-start.13 = (f32[4,1,32,128]{3,2,1,0:T(8,128)S(1)}, f32[4,1,32,128]{3,2,1,0:T(8,128)S(1)}, u32[]{:S(2)}, u32[]{:S(2)}) collective-permute-start(f32[4,1,32,128]{3,2,1,0:T(8,128)S(1)} %get-tuple-element.328), channel_id=1, source_target_pairs={{0,2},{2,4},{4,6},{6,8},{8,10},{10,12},{12,14},{14,16},{16,18},{18... | collective-permute-start | bytes 196616 | tf_op jit(solution)/shard_map/ppermute | solution.py:22
  93.8 4.5 collective-permute-done.12
  105.4 280.4 %while.32 = (s32[]{:T(128)}, f32[4,1,4,16]{3,2,1,0:T(4,128)S(1)}, f32[4,1,4,16]{3,2,1,0:T(4,128)S(1)}, f32[4,1,4,16]{3,2,1,0:T(4,128)S(1)}, f32[4,16]{1,0:T(4,128)S(1)}, /*index=5*/f32[4]{0:T(128)S(1)}, s32[]{:T(128)}, s32[]{:T(128)}) while((s32[]{:T(128)}, f32[4,1,4,16]{3,2,1,0:T(4,128)S(1)}, f32[4,1,4,16]{3,2,1,0:T(4,128)S(1)}, ...), condition=%wide.region_7.8_spmd.clone, body=%wide.region_6.7_spmd.clone.sunk | while | flops 5123 | bytes 34959 | solution.py:99
  105.5 5.5 %collective-permute-start.1 = (f32[4,1,4,16]{3,2,1,0:T(4,128)S(1)}, f32[4,1,4,16]{3,2,1,0:T(4,128)S(1)}, u32[]{:S(2)}, u32[]{:S(2)}) collective-permute-start(f32[4,1,4,16]{3,2,1,0:T(4,128)S(1)} %broadcast_select_fusion.2), channel_id=1, source_target_pairs={{0,2},{2,4},{4,6},{6,8},{8,10},{10,12},{12,14},{14,16},{16,18},{18... | collective-permute-start | bytes 3080 | tf_op jit(solution)/shard_map/while/body/eval_jaxpr/ppermute | solution.py:22
  112.3 4.2 collective-permute-done
  121.0 4.5 collective-permute-start.1
  126.8 4.2 collective-permute-done
  140.9 4.2 collective-permute-done
  154.6 4.2 collective-permute-done
  168.7 4.2 collective-permute-done
  177.3 4.5 collective-permute-start.1
  183.2 4.2 collective-permute-done
  197.2 4.2 collective-permute-done
  211.0 4.2 collective-permute-done
  225.0 4.2 collective-permute-done
  233.7 4.5 collective-permute-start.1
  239.6 4.2 collective-permute-done
  253.6 4.2 collective-permute-done
  267.3 4.2 collective-permute-done
  281.1 4.2 collective-permute-done
  294.8 4.2 collective-permute-done
  308.5 4.2 collective-permute-done
  322.3 4.2 collective-permute-done
  336.0 4.2 collective-permute-done
  349.7 4.2 collective-permute-done
  363.5 4.2 collective-permute-done
  391.1 10.1 %collective-permute-done.17 = f32[4,1,32,128]{2,3,0,1:T(8,128)S(1)} collective-permute-done((f32[4,1,32,128]{2,3,0,1:T(8,128)S(1)}, f32[4,1,32,128]{2,3,0,1:T(8,128)S(1)}, u32[]{:S(2)}, u32[]{:S(2)}) %collective-permute-start.17) | collective-permute-done | bytes 65568 | tf_op jit(solution)/shard_map/ppermute | solution.py:22
  405.3 4.2 collective-permute-start.19
  412.4 38.1 %all-reduce.50 = (f32[4]{0:T(128)S(1)}, f32[4]{0:T(128)S(1)}) all-reduce(f32[4]{0:T(128)S(1)} %get-tuple-element.286, f32[4]{0:T(128)S(1)} %get-tuple-element.285), channel_id=1, replica_groups=mesh['span'=16,'width'=2] {'span','width'}, use_global_device_ids=true, to_apply=%region_9.10 | all-reduce | flops 8 | bytes 64 | tf_op jit(solution)/shard_map/psum | solution.py:105
  457.6 4.3 collective-permute-done.20
  (389 shorter events, 290.6 us)
Async XLA Ops:
  1.5 10.2 %collective-permute-start.4 = (f32[4,1,32,128]{3,2,1,0:T(8,128)S(1)}, f32[4,1,32,128]{3,2,1,0:T(8,128)S(1)}, u32[]{:S(2)}, u32[]{:S(2)}) collective-permute-start(f32[4,1,32,128]{3,2,1,0:T(8,128)S(1)} %get-tuple-element.364), channel_id=1, source_target_pairs={{2,0},{4,2},{6,4},{8,6},{10,8},{12,10},{14,12},{16,14},{18,16},{20... | collective-permute-start | bytes 196616 | tf_op jit(solution)/shard_map/ppermute | solution.py:23
  2.8 8.1 %collective-permute-start.5 = (f32[4,1,32,128]{3,2,1,0:T(8,128)S(1)}, f32[4,1,32,128]{3,2,1,0:T(8,128)S(1)}, u32[]{:S(2)}, u32[]{:S(2)}) collective-permute-start(f32[4,1,32,128]{3,2,1,0:T(8,128)S(1)} %get-tuple-element.365), channel_id=1, source_target_pairs={{0,2},{2,4},{4,6},{6,8},{8,10},{10,12},{12,14},{14,16},{16,18},{18... | collective-permute-start | bytes 196616 | tf_op jit(solution)/shard_map/ppermute | solution.py:22
  23.3 7.2 %collective-permute-start.8 = (f32[4,1,32,128]{3,2,1,0:T(8,128)}, f32[4,1,32,128]{3,2,1,0:T(8,128)S(1)}, u32[]{:S(2)}, u32[]{:S(2)}) collective-permute-start(f32[4,1,32,128]{3,2,1,0:T(8,128)} %get-tuple-element.348), channel_id=1, source_target_pairs={{0,2},{2,4},{4,6},{6,8},{8,10},{10,12},{12,14},{14,16},{16,18},{18... | collective-permute-start | bytes 196616 | tf_op jit(solution)/shard_map/ppermute | solution.py:22
  28.2 6.5 %collective-permute-start.9 = (f32[4,1,32,128]{3,2,1,0:T(8,128)}, f32[4,1,32,128]{3,2,1,0:T(8,128)}, u32[]{:S(2)}, u32[]{:S(2)}) collective-permute-start(f32[4,1,32,128]{3,2,1,0:T(8,128)} %get-tuple-element.349), channel_id=1, source_target_pairs={{2,0},{4,2},{6,4},{8,6},{10,8},{12,10},{14,12},{16,14},{18,16},{20... | collective-permute-start | bytes 196616 | tf_op jit(solution)/shard_map/ppermute | solution.py:23
  86.9 6.9 %collective-permute-start.13 = (f32[4,1,32,128]{3,2,1,0:T(8,128)S(1)}, f32[4,1,32,128]{3,2,1,0:T(8,128)S(1)}, u32[]{:S(2)}, u32[]{:S(2)}) collective-permute-start(f32[4,1,32,128]{3,2,1,0:T(8,128)S(1)} %get-tuple-element.328), channel_id=1, source_target_pairs={{0,2},{2,4},{4,6},{6,8},{8,10},{10,12},{12,14},{14,16},{16,18},{18... | collective-permute-start | bytes 196616 | tf_op jit(solution)/shard_map/ppermute | solution.py:22
  91.7 6.6 %collective-permute-start.12 = (f32[4,1,32,128]{3,2,1,0:T(8,128)S(1)}, f32[4,1,32,128]{3,2,1,0:T(8,128)S(1)}, u32[]{:S(2)}, u32[]{:S(2)}) collective-permute-start(f32[4,1,32,128]{3,2,1,0:T(8,128)S(1)} %get-tuple-element.329), channel_id=1, source_target_pairs={{2,0},{4,2},{6,4},{8,6},{10,8},{12,10},{14,12},{16,14},{18,16},{20... | collective-permute-start | bytes 196616 | tf_op jit(solution)/shard_map/ppermute | solution.py:23
  105.5 6.8 %collective-permute-start.1 = (f32[4,1,4,16]{3,2,1,0:T(4,128)S(1)}, f32[4,1,4,16]{3,2,1,0:T(4,128)S(1)}, u32[]{:S(2)}, u32[]{:S(2)}) collective-permute-start(f32[4,1,4,16]{3,2,1,0:T(4,128)S(1)} %broadcast_select_fusion.2), channel_id=1, source_target_pairs={{0,2},{2,4},{4,6},{6,8},{8,10},{10,12},{12,14},{14,16},{16,18},{18... | collective-permute-start | bytes 3080 | tf_op jit(solution)/shard_map/while/body/eval_jaxpr/ppermute | solution.py:22
  110.9 5.5 %collective-permute-start = (f32[4,1,4,16]{3,2,1,0:T(4,128)S(1)}, f32[4,1,4,16]{3,2,1,0:T(4,128)S(1)}, u32[]{:S(2)}, u32[]{:S(2)}) collective-permute-start(f32[4,1,4,16]{3,2,1,0:T(4,128)S(1)} %broadcast_select_fusion.2), channel_id=1, source_target_pairs={{2,0},{4,2},{6,4},{8,6},{10,8},{12,10},{14,12},{16,14},{18,16},{20... | collective-permute-start | bytes 3080 | tf_op jit(solution)/shard_map/while/body/eval_jaxpr/ppermute | solution.py:23
  121.0 5.9 %collective-permute-start.1 = (f32[4,1,4,16]{3,2,1,0:T(4,128)S(1)}, f32[4,1,4,16]{3,2,1,0:T(4,128)S(1)}, u32[]{:S(2)}, u32[]{:S(2)}) collective-permute-start(f32[4,1,4,16]{3,2,1,0:T(4,128)S(1)} %broadcast_select_fusion.2), channel_id=1, source_target_pairs={{0,2},{2,4},{4,6},{6,8},{8,10},{10,12},{12,14},{14,16},{16,18},{18... | collective-permute-start | bytes 3080 | tf_op jit(solution)/shard_map/while/body/eval_jaxpr/ppermute | solution.py:22
  125.5 5.5 %collective-permute-start = (f32[4,1,4,16]{3,2,1,0:T(4,128)S(1)}, f32[4,1,4,16]{3,2,1,0:T(4,128)S(1)}, u32[]{:S(2)}, u32[]{:S(2)}) collective-permute-start(f32[4,1,4,16]{3,2,1,0:T(4,128)S(1)} %broadcast_select_fusion.2), channel_id=1, source_target_pairs={{2,0},{4,2},{6,4},{8,6},{10,8},{12,10},{14,12},{16,14},{18,16},{20... | collective-permute-start | bytes 3080 | tf_op jit(solution)/shard_map/while/body/eval_jaxpr/ppermute | solution.py:23
  139.5 5.5 %collective-permute-start = (f32[4,1,4,16]{3,2,1,0:T(4,128)S(1)}, f32[4,1,4,16]{3,2,1,0:T(4,128)S(1)}, u32[]{:S(2)}, u32[]{:S(2)}) collective-permute-start(f32[4,1,4,16]{3,2,1,0:T(4,128)S(1)} %broadcast_select_fusion.2), channel_id=1, source_target_pairs={{2,0},{4,2},{6,4},{8,6},{10,8},{12,10},{14,12},{16,14},{18,16},{20... | collective-permute-start | bytes 3080 | tf_op jit(solution)/shard_map/while/body/eval_jaxpr/ppermute | solution.py:23
  153.2 5.5 %collective-permute-start = (f32[4,1,4,16]{3,2,1,0:T(4,128)S(1)}, f32[4,1,4,16]{3,2,1,0:T(4,128)S(1)}, u32[]{:S(2)}, u32[]{:S(2)}) collective-permute-start(f32[4,1,4,16]{3,2,1,0:T(4,128)S(1)} %broadcast_select_fusion.2), channel_id=1, source_target_pairs={{2,0},{4,2},{6,4},{8,6},{10,8},{12,10},{14,12},{16,14},{18,16},{20... | collective-permute-start | bytes 3080 | tf_op jit(solution)/shard_map/while/body/eval_jaxpr/ppermute | solution.py:23
  167.3 5.5 %collective-permute-start = (f32[4,1,4,16]{3,2,1,0:T(4,128)S(1)}, f32[4,1,4,16]{3,2,1,0:T(4,128)S(1)}, u32[]{:S(2)}, u32[]{:S(2)}) collective-permute-start(f32[4,1,4,16]{3,2,1,0:T(4,128)S(1)} %broadcast_select_fusion.2), channel_id=1, source_target_pairs={{2,0},{4,2},{6,4},{8,6},{10,8},{12,10},{14,12},{16,14},{18,16},{20... | collective-permute-start | bytes 3080 | tf_op jit(solution)/shard_map/while/body/eval_jaxpr/ppermute | solution.py:23
  177.3 5.9 %collective-permute-start.1 = (f32[4,1,4,16]{3,2,1,0:T(4,128)S(1)}, f32[4,1,4,16]{3,2,1,0:T(4,128)S(1)}, u32[]{:S(2)}, u32[]{:S(2)}) collective-permute-start(f32[4,1,4,16]{3,2,1,0:T(4,128)S(1)} %broadcast_select_fusion.2), channel_id=1, source_target_pairs={{0,2},{2,4},{4,6},{6,8},{8,10},{10,12},{12,14},{14,16},{16,18},{18... | collective-permute-start | bytes 3080 | tf_op jit(solution)/shard_map/while/body/eval_jaxpr/ppermute | solution.py:22
  181.9 5.5 %collective-permute-start = (f32[4,1,4,16]{3,2,1,0:T(4,128)S(1)}, f32[4,1,4,16]{3,2,1,0:T(4,128)S(1)}, u32[]{:S(2)}, u32[]{:S(2)}) collective-permute-start(f32[4,1,4,16]{3,2,1,0:T(4,128)S(1)} %broadcast_select_fusion.2), channel_id=1, source_target_pairs={{2,0},{4,2},{6,4},{8,6},{10,8},{12,10},{14,12},{16,14},{18,16},{20... | collective-permute-start | bytes 3080 | tf_op jit(solution)/shard_map/while/body/eval_jaxpr/ppermute | solution.py:23
  195.9 5.5 %collective-permute-start = (f32[4,1,4,16]{3,2,1,0:T(4,128)S(1)}, f32[4,1,4,16]{3,2,1,0:T(4,128)S(1)}, u32[]{:S(2)}, u32[]{:S(2)}) collective-permute-start(f32[4,1,4,16]{3,2,1,0:T(4,128)S(1)} %broadcast_select_fusion.2), channel_id=1, source_target_pairs={{2,0},{4,2},{6,4},{8,6},{10,8},{12,10},{14,12},{16,14},{18,16},{20... | collective-permute-start | bytes 3080 | tf_op jit(solution)/shard_map/while/body/eval_jaxpr/ppermute | solution.py:23
  209.6 5.5 %collective-permute-start = (f32[4,1,4,16]{3,2,1,0:T(4,128)S(1)}, f32[4,1,4,16]{3,2,1,0:T(4,128)S(1)}, u32[]{:S(2)}, u32[]{:S(2)}) collective-permute-start(f32[4,1,4,16]{3,2,1,0:T(4,128)S(1)} %broadcast_select_fusion.2), channel_id=1, source_target_pairs={{2,0},{4,2},{6,4},{8,6},{10,8},{12,10},{14,12},{16,14},{18,16},{20... | collective-permute-start | bytes 3080 | tf_op jit(solution)/shard_map/while/body/eval_jaxpr/ppermute | solution.py:23
  223.7 5.5 %collective-permute-start = (f32[4,1,4,16]{3,2,1,0:T(4,128)S(1)}, f32[4,1,4,16]{3,2,1,0:T(4,128)S(1)}, u32[]{:S(2)}, u32[]{:S(2)}) collective-permute-start(f32[4,1,4,16]{3,2,1,0:T(4,128)S(1)} %broadcast_select_fusion.2), channel_id=1, source_target_pairs={{2,0},{4,2},{6,4},{8,6},{10,8},{12,10},{14,12},{16,14},{18,16},{20... | collective-permute-start | bytes 3080 | tf_op jit(solution)/shard_map/while/body/eval_jaxpr/ppermute | solution.py:23
  233.7 5.9 %collective-permute-start.1 = (f32[4,1,4,16]{3,2,1,0:T(4,128)S(1)}, f32[4,1,4,16]{3,2,1,0:T(4,128)S(1)}, u32[]{:S(2)}, u32[]{:S(2)}) collective-permute-start(f32[4,1,4,16]{3,2,1,0:T(4,128)S(1)} %broadcast_select_fusion.2), channel_id=1, source_target_pairs={{0,2},{2,4},{4,6},{6,8},{8,10},{10,12},{12,14},{14,16},{16,18},{18... | collective-permute-start | bytes 3080 | tf_op jit(solution)/shard_map/while/body/eval_jaxpr/ppermute | solution.py:22
  238.2 5.5 %collective-permute-start = (f32[4,1,4,16]{3,2,1,0:T(4,128)S(1)}, f32[4,1,4,16]{3,2,1,0:T(4,128)S(1)}, u32[]{:S(2)}, u32[]{:S(2)}) collective-permute-start(f32[4,1,4,16]{3,2,1,0:T(4,128)S(1)} %broadcast_select_fusion.2), channel_id=1, source_target_pairs={{2,0},{4,2},{6,4},{8,6},{10,8},{12,10},{14,12},{16,14},{18,16},{20... | collective-permute-start | bytes 3080 | tf_op jit(solution)/shard_map/while/body/eval_jaxpr/ppermute | solution.py:23
  266.0 5.5 %collective-permute-start = (f32[4,1,4,16]{3,2,1,0:T(4,128)S(1)}, f32[4,1,4,16]{3,2,1,0:T(4,128)S(1)}, u32[]{:S(2)}, u32[]{:S(2)}) collective-permute-start(f32[4,1,4,16]{3,2,1,0:T(4,128)S(1)} %broadcast_select_fusion.2), channel_id=1, source_target_pairs={{2,0},{4,2},{6,4},{8,6},{10,8},{12,10},{14,12},{16,14},{18,16},{20... | collective-permute-start | bytes 3080 | tf_op jit(solution)/shard_map/while/body/eval_jaxpr/ppermute | solution.py:23
  293.4 5.5 %collective-permute-start = (f32[4,1,4,16]{3,2,1,0:T(4,128)S(1)}, f32[4,1,4,16]{3,2,1,0:T(4,128)S(1)}, u32[]{:S(2)}, u32[]{:S(2)}) collective-permute-start(f32[4,1,4,16]{3,2,1,0:T(4,128)S(1)} %broadcast_select_fusion.2), channel_id=1, source_target_pairs={{2,0},{4,2},{6,4},{8,6},{10,8},{12,10},{14,12},{16,14},{18,16},{20... | collective-permute-start | bytes 3080 | tf_op jit(solution)/shard_map/while/body/eval_jaxpr/ppermute | solution.py:23
  320.9 5.5 %collective-permute-start = (f32[4,1,4,16]{3,2,1,0:T(4,128)S(1)}, f32[4,1,4,16]{3,2,1,0:T(4,128)S(1)}, u32[]{:S(2)}, u32[]{:S(2)}) collective-permute-start(f32[4,1,4,16]{3,2,1,0:T(4,128)S(1)} %broadcast_select_fusion.2), channel_id=1, source_target_pairs={{2,0},{4,2},{6,4},{8,6},{10,8},{12,10},{14,12},{16,14},{18,16},{20... | collective-permute-start | bytes 3080 | tf_op jit(solution)/shard_map/while/body/eval_jaxpr/ppermute | solution.py:23
  334.7 5.5 %collective-permute-start = (f32[4,1,4,16]{3,2,1,0:T(4,128)S(1)}, f32[4,1,4,16]{3,2,1,0:T(4,128)S(1)}, u32[]{:S(2)}, u32[]{:S(2)}) collective-permute-start(f32[4,1,4,16]{3,2,1,0:T(4,128)S(1)} %broadcast_select_fusion.2), channel_id=1, source_target_pairs={{2,0},{4,2},{6,4},{8,6},{10,8},{12,10},{14,12},{16,14},{18,16},{20... | collective-permute-start | bytes 3080 | tf_op jit(solution)/shard_map/while/body/eval_jaxpr/ppermute | solution.py:23
  348.4 5.5 %collective-permute-start = (f32[4,1,4,16]{3,2,1,0:T(4,128)S(1)}, f32[4,1,4,16]{3,2,1,0:T(4,128)S(1)}, u32[]{:S(2)}, u32[]{:S(2)}) collective-permute-start(f32[4,1,4,16]{3,2,1,0:T(4,128)S(1)} %broadcast_select_fusion.2), channel_id=1, source_target_pairs={{2,0},{4,2},{6,4},{8,6},{10,8},{12,10},{14,12},{16,14},{18,16},{20... | collective-permute-start | bytes 3080 | tf_op jit(solution)/shard_map/while/body/eval_jaxpr/ppermute | solution.py:23
  362.1 5.5 %collective-permute-start = (f32[4,1,4,16]{3,2,1,0:T(4,128)S(1)}, f32[4,1,4,16]{3,2,1,0:T(4,128)S(1)}, u32[]{:S(2)}, u32[]{:S(2)}) collective-permute-start(f32[4,1,4,16]{3,2,1,0:T(4,128)S(1)} %broadcast_select_fusion.2), channel_id=1, source_target_pairs={{2,0},{4,2},{6,4},{8,6},{10,8},{12,10},{14,12},{16,14},{18,16},{20... | collective-permute-start | bytes 3080 | tf_op jit(solution)/shard_map/while/body/eval_jaxpr/ppermute | solution.py:23
  375.9 5.5 %collective-permute-start = (f32[4,1,4,16]{3,2,1,0:T(4,128)S(1)}, f32[4,1,4,16]{3,2,1,0:T(4,128)S(1)}, u32[]{:S(2)}, u32[]{:S(2)}) collective-permute-start(f32[4,1,4,16]{3,2,1,0:T(4,128)S(1)} %broadcast_select_fusion.2), channel_id=1, source_target_pairs={{2,0},{4,2},{6,4},{8,6},{10,8},{12,10},{14,12},{16,14},{18,16},{20... | collective-permute-start | bytes 3080 | tf_op jit(solution)/shard_map/while/body/eval_jaxpr/ppermute | solution.py:23
  386.0 15.2 %collective-permute-start.17 = (f32[4,1,32,128]{2,3,0,1:T(8,128)S(1)}, f32[4,1,32,128]{2,3,0,1:T(8,128)S(1)}, u32[]{:S(2)}, u32[]{:S(2)}) collective-permute-start(f32[4,1,32,128]{2,3,0,1:T(8,128)S(1)} %get-tuple-element.370), channel_id=1, source_target_pairs={{0,2},{2,4},{4,6},{6,8},{8,10},{10,12},{12,14},{14,16},{16,18},{18... | collective-permute-start | bytes 196616 | tf_op jit(solution)/shard_map/ppermute | solution.py:22
  389.7 12.8 %collective-permute-start.16 = (f32[4,1,32,128]{2,3,0,1:T(8,128)S(1)}, f32[4,1,32,128]{2,3,0,1:T(8,128)S(1)}, u32[]{:S(2)}, u32[]{:S(2)}) collective-permute-start(f32[4,1,32,128]{2,3,0,1:T(8,128)S(1)} %get-tuple-element.370), channel_id=1, source_target_pairs={{2,0},{4,2},{6,4},{8,6},{10,8},{12,10},{14,12},{16,14},{18,16},{20... | collective-permute-start | bytes 196616 | tf_op jit(solution)/shard_map/ppermute | solution.py:23
  404.0 5.8 %collective-permute-start.18 = (f32[4,10,1,128]{3,2,1,0:T(1,128)}, f32[4,10,1,128]{3,2,1,0:T(1,128)}, u32[]{:S(2)}, u32[]{:S(2)}) collective-permute-start(f32[4,10,1,128]{3,2,1,0:T(1,128)} %get-tuple-element.314), channel_id=1, source_target_pairs={{1,0},{3,2},{5,4},{7,6},{9,8},{11,10},{13,12},{15,14},{17,16},{19,... | collective-permute-start | bytes 61448 | tf_op jit(solution)/shard_map/ppermute | solution.py:23
  451.5 6.1 %collective-permute-start.21 = (f32[4,1,32,128]{3,2,1,0:T(8,128)S(1)}, f32[4,1,32,128]{3,2,1,0:T(8,128)S(1)}, u32[]{:S(2)}, u32[]{:S(2)}) collective-permute-start(f32[4,1,32,128]{3,2,1,0:T(8,128)S(1)} %get-tuple-element.324), channel_id=1, source_target_pairs={{0,2},{2,4},{4,6},{6,8},{8,10},{10,12},{12,14},{14,16},{16,18},{18... | collective-permute-start | bytes 196616 | tf_op jit(solution)/shard_map/ppermute | solution.py:22
  455.7 6.2 %collective-permute-start.20 = (f32[4,1,32,128]{3,2,1,0:T(8,128)S(1)}, f32[4,1,32,128]{3,2,1,0:T(8,128)S(1)}, u32[]{:S(2)}, u32[]{:S(2)}) collective-permute-start(f32[4,1,32,128]{3,2,1,0:T(8,128)S(1)} %get-tuple-element.325), channel_id=1, source_target_pairs={{2,0},{4,2},{6,4},{8,6},{10,8},{12,10},{14,12},{16,14},{18,16},{20... | collective-permute-start | bytes 196616 | tf_op jit(solution)/shard_map/ppermute | solution.py:23
  (89 other events, 334.1 us)
where the time goes:
time: 472 us; the launch traced here: 468 us
  starting transfers between devices  208 us (44%)
  waiting for transfers between devices  147 us (31%)
  local copies, waits for them, and re-layouts  53 us (11%)
  blocking collectives  38.1 us (8%)
  other arithmetic  19.2 us (4%)
    ppermute x50, starting transfers between devices, padded(): before = lax.ppermute(last, axis, up)  143 us
    ppermute x50, waiting for transfers between devices, padded(): after = lax.ppermute(first, axis, down)  132 us
    ppermute x50, starting transfers between devices, padded(): after = lax.ppermute(first, axis, down)  64.8 us
    psum x1, blocking collectives, on_device(): lax.psum((jnp.sum(fine * image, axis=(1, 2, 3)), jnp.sum(image * image, a...  38.1 us
    scatter x9, local copies, waits for them, and re-layouts, on_device(): full = frozen.at[:, 1:-1, 1:-1, :].set(delta)  26.2 us
    unnamed x50, local copies, waits for them, and re-layouts  15.6 us
    ppermute x50, waiting for transfers between devices, padded(): before = lax.ppermute(last, axis, up)  14.8 us
  transfers between devices with their start and end apart: 100, of which 53 were waited for; matrix products, arithmetic and copies ran while one was open for 1% of the time, Pallas kernels for 0%

commit v1 on v0

v1 whole, which is shorter than its diff:
```python
import functools

import jax
import jax.numpy as jnp
from jax import lax
from jax.experimental import pallas as pl
from jax.experimental.pallas import tpu as pltpu
from jax.sharding import PartitionSpec as P

COARSEN = 8
SWEEPS = 4
COARSE_ITERS = 20
INV_STEP = 0.05
EPSILON = 1e-06
MESH = pl.DeviceIdType.MESH
F32 = jnp.float32


def kernel(
    n_span, n_width, ions, cx, cy, cz,
    state_ref, source_ref, cond_ref, cover_ref, colour_ref, spread_ref, strength_ref,
    up_ref, res_ref,
    xs, xh, ys, yh, gath, part, condp, coverp, rhs, diag, c, a, d, image,
    mx, fx, cx_sum, aj, cj, ej, sp, wv,
    send_sem, recv_sem, gsend, grecv, psend, precv,
):
    s = lax.axis_index("span")
    w = lax.axis_index("width")
    total_dev = n_span * n_width
    me = s * n_width + w
    kp = cx // 2
    rows = cy // COARSEN
    row = lax.broadcasted_iota(jnp.int32, (cy, cz), 0)
    lane = lax.broadcasted_iota(jnp.int32, (cy, cz), 1)
    p = (row + lane) % 2 == 1
    first_y, last_y = row == 0, row == cy - 1
    first_z, last_z = lane == 0, lane == cz - 1

    barrier = pltpu.get_barrier_semaphore()

    def partner(off):
        other = lax.rem(me + off, total_dev)
        return (other // n_width, other % n_width)

    @pl.loop(1, total_dev)
    def _(off):
        pl.semaphore_signal(barrier, inc=1, device_id=partner(off), device_id_type=MESH)

    def split(x):
        pairs = x.reshape(kp, 2, cy, cz)
        even, odd = pairs[:, 0], pairs[:, 1]
        return jnp.where(p, odd, even), jnp.where(p, even, odd)

    def yz_sum(v):
        out = jnp.where(last_y, 0.0, pltpu.roll(v, cy - 1, v.ndim - 2))
        out += jnp.where(first_y, 0.0, pltpu.roll(v, 1, v.ndim - 2))
        out += jnp.where(last_z, 0.0, pltpu.roll(v, cz - 1, v.ndim - 1))
        out += jnp.where(first_z, 0.0, pltpu.roll(v, 1, v.ndim - 1))
        return out

    zero_face = jnp.zeros((1, cy, cz), F32)

    def nb_red(black):
        above = jnp.concatenate([black[1:], zero_face], axis=0)
        below = jnp.concatenate([zero_face, black[:-1]], axis=0)
        return black + jnp.where(p, above, below) + yz_sum(black)

    def nb_black(red):
        above = jnp.concatenate([red[1:], zero_face], axis=0)
        below = jnp.concatenate([zero_face, red[:-1]], axis=0)
        return red + jnp.where(p, below, above) + yz_sum(red)

    def rim(e, i):
        lo, hi = xh[e, 0, i], xh[e, 1, i]
        ylo, yhi = yh[e, 0, i], yh[e, 1, i]
        mid = jnp.zeros((kp - 2, cy, cz), F32)

        def faces(k0, k1, half):
            x_part = jnp.concatenate([k0[None], mid, k1[None]], axis=0)
            low = ylo[half * kp:(half + 1) * kp][:, None, :]
            high = yhi[half * kp:(half + 1) * kp][:, None, :]
            return x_part + jnp.where(first_y, low, 0.0) + jnp.where(last_y, high, 0.0)

        red = faces(jnp.where(p, 0.0, lo), jnp.where(p, hi, 0.0), 1)
        black = faces(jnp.where(p, lo, 0.0), jnp.where(p, 0.0, hi), 0)
        return red, black

    def put_y(e, i, red, black):
        ys[e, 0, i] = jnp.concatenate([red[:, cy - 1, :], black[:, cy - 1, :]], axis=0)
        ys[e, 1, i] = jnp.concatenate([red[:, 0, :], black[:, 0, :]], axis=0)

    def put_x(e, i, red, black):
        xs[e - 1, 0, i] = jnp.where(p, red[kp - 1], black[kp - 1])
        xs[e - 1, 1, i] = jnp.where(p, black[0], red[0])

    has = (s < n_span - 1, s > 0, w < n_width - 1, w > 0)
    gets = (s > 0, s < n_span - 1, w > 0, w < n_width - 1)
    to = ((s + 1, w), (s - 1, w), (s, w + 1), (s, w - 1))

    def copy(e, k):
        if k >= 2:
            src, dst = ys.at[e, k - 2], yh.at[e, k - 2]
        else:
            dst = xh.at[e, k]
            if e == 0:
                src = state_ref.at[:, cx - 1] if k == 0 else state_ref.at[:, 0]
            else:
                src = xs.at[e - 1, k]
        return pltpu.make_async_remote_copy(
            src_ref=src, dst_ref=dst, send_sem=send_sem.at[e, k], recv_sem=recv_sem.at[e, k],
            device_id=to[k], device_id_type=MESH,
        )

    def send(e, which):
        for k in which:
            @pl.when(has[k])
            def _():
                copy(e, k).start()

    def receive(e):
        for k in range(4):
            @pl.when(gets[k])
            def _():
                copy(e, k).wait_recv()

    for k in range(4):
        @pl.when(jnp.logical_not(gets[k]))
        def _():
            for e in range(3):
                if k >= 2:
                    yh[e, k - 2] = jnp.zeros(yh.shape[2:], F32)
                else:
                    xh[e, k] = jnp.zeros(xh.shape[2:], F32)

    def pack_state(i, _):
        put_y(0, i, *split(state_ref[i]))
        return 0

    lax.fori_loop(0, ions, pack_state, 0)
    pl.semaphore_wait(barrier, total_dev - 1)
    send(0, range(4))

    condp[0], condp[1] = split(cond_ref[...])
    coverp[0], coverp[1] = split(cover_ref[...].astype(F32))
    cx_sum[...] = jnp.sum(cond_ref[...], axis=0)

    def local_terms(i, _):
        spread, strength = spread_ref[i], strength_ref[i]
        st = split(state_ref[i])
        src = split(source_ref[i])
        near = (nb_red(st[1]), nb_black(st[0]))
        mass_sum = jnp.zeros((cy, cz), F32)
        for h in range(2):
            coef = spread * condp[h]
            inv = 1.0 / (1.0 + st[h])
            bound = coverp[h] * strength * inv
            mass = INV_STEP + bound * inv
            dg = mass + 6.0 * coef
            diag[h, i] = dg
            c[h, i] = coef / dg
            rhs[h, i] = src[h] - (coef * (6.0 * st[h] - near[h]) + bound * st[h])
            mass_sum += jnp.sum(mass, axis=0)
        mx[i] = mass_sum
        return 0

    lax.fori_loop(0, ions, local_terms, 0)
    receive(0)

    mine = colour_ref[0, 0].astype(F32)

    def sweeps(ar, ab, cr, cb):
        red = ar
        black = ab + cb * nb_black(red)
        for _ in range(SWEEPS - 1):
            red = ar + cr * nb_red(black)
            black = ab + cb * nb_black(red)
        return red, black

    def phase_zero(i, _):
        near = rim(0, i)
        for h in range(2):
            right = rhs[h, i] + spread_ref[i] * condp[h] * near[h]
            rhs[h, i] = right
            a[h, i] = right / diag[h, i]
        red, black = sweeps(
            (1.0 - mine) * a[0, i], (1.0 - mine) * a[1, i], c[0, i], c[1, i]
        )
        d[0, i], d[1, i] = red, black
        put_y(1, i, red, black)
        put_x(1, i, red, black)
        return 0

    lax.fori_loop(0, ions, phase_zero, 0)
    send(1, range(4))
    receive(1)

    def phase_one(i, _):
        near = rim(1, i)
        red, black = sweeps(
            mine * (a[0, i] + c[0, i] * near[0]), mine * (a[1, i] + c[1, i] * near[1]),
            c[0, i], c[1, i],
        )
        red, black = red + d[0, i], black + d[1, i]
        d[0, i], d[1, i] = red, black
        put_y(2, i, red, black)
        put_x(2, i, red, black)
        return 0

    lax.fori_loop(0, ions, phase_one, 0)
    send(2, range(4))

    eighth = lane % COARSEN

    def coarse_pack(parts):
        acc = jnp.zeros((cy, cz), F32)
        for i in range(ions):
            v = parts[i]
            for step in (1, 2, 4):
                v = v + pltpu.roll(v, cz - step, 1)
            if i:
                v = pltpu.roll(v, i, 1)
            acc = jnp.where(eighth == i, v, acc)
        return jnp.concatenate(
            [jnp.sum(acc[j * COARSEN:(j + 1) * COARSEN], axis=0, keepdims=True)
             for j in range(rows)], axis=0)

    cond_sum = cx_sum[...]
    coarse_off = coarse_pack([spread_ref[i] * cond_sum for i in range(ions)]) / COARSEN
    coarse_diag = coarse_pack([mx[i] for i in range(ions)]) + 6.0 * coarse_off
    coarse_inv = 1.0 / jnp.where(eighth[:rows] < ions, coarse_diag, 1.0)

    receive(2)

    def fine_terms(i, _):
        near = rim(2, i)
        red, black = d[0, i], d[1, i]
        near = (near[0] + nb_red(black), near[1] + nb_black(red))
        total = jnp.zeros((cy, cz), F32)
        for h, v in ((0, red), (1, black)):
            fine = rhs[h, i] - (diag[h, i] * v - spread_ref[i] * condp[h] * near[h])
            rhs[h, i] = fine
            total += jnp.sum(fine, axis=0)
        fx[i] = total
        return 0

    lax.fori_loop(0, ions, fine_terms, 0)
    crhs = coarse_pack([fx[i] for i in range(ions)])
    gath[me] = jnp.concatenate([crhs * coarse_inv, coarse_off * coarse_inv], axis=0)

    def spread_out(buf, ssem, rsem):
        @pl.loop(1, total_dev)
        def _(off):
            pltpu.make_async_remote_copy(
                src_ref=buf.at[me], dst_ref=buf.at[me], send_sem=ssem, recv_sem=rsem,
                device_id=partner(off), device_id_type=MESH,
            ).start()

    def all_of(buf, sem):
        others = buf.at[pl.ds(0, total_dev - 1)]
        pltpu.make_async_copy(others, others, sem).wait()

    spread_out(gath, gsend, grecv)
    all_of(gath, grecv)

    wide = n_width * rows
    g = gath[...].reshape(n_span, n_width, 2 * rows, cz)
    aj[...] = jnp.concatenate([g[:, k, :rows] for k in range(n_width)], axis=1)
    cj[...] = jnp.concatenate([g[:, k, rows:] for k in range(n_width)], axis=1)
    crow = lax.broadcasted_iota(jnp.int32, (wide, cz), 0)
    clane = lax.broadcasted_iota(jnp.int32, (wide, cz), 1)
    zero_c = jnp.zeros((1, wide, cz), F32)

    def jacobi(_, e):
        total = jnp.concatenate([e[1:], zero_c], axis=0)
        total += jnp.concatenate([zero_c, e[:-1]], axis=0)
        total += jnp.where(crow == wide - 1, 0.0, pltpu.roll(e, wide - 1, 1))
        total += jnp.where(crow == 0, 0.0, pltpu.roll(e, 1, 1))
        total += jnp.where(clane >= cz - COARSEN, 0.0, pltpu.roll(e, cz - COARSEN, 2))
        total += jnp.where(clane < COARSEN, 0.0, pltpu.roll(e, COARSEN, 2))
        return aj[...] + cj[...] * total

    e = lax.fori_loop(0, COARSE_ITERS - 1, jacobi, aj[...])
    ej[0] = zero_c[0]
    ej[n_span + 1] = zero_c[0]
    ej[1:n_span + 1] = e
    before, here, after = ej[s], ej[s + 1], ej[s + 2]

    def own_rows(v):
        out = v[:rows]
        for k in range(1, n_width):
            out = jnp.where(w == k, v[k * rows:(k + 1) * rows], out)
        return out

    y_low = jnp.zeros((1, cz), F32)
    y_high = jnp.zeros((1, cz), F32)
    for k in range(n_width):
        if k > 0:
            y_low = jnp.where(w == k, here[k * rows - 1:k * rows], y_low)
        if k < n_width - 1:
            y_high = jnp.where(w == k, here[(k + 1) * rows:(k + 1) * rows + 1], y_high)
    packed = jnp.concatenate(
        [own_rows(here), own_rows(before), own_rows(after), y_low, y_high,
         jnp.zeros((16 - 3 * rows - 2, cz), F32)], axis=0)
    for i in range(ions):
        v = jnp.where(eighth[:16] == i, packed, 0.0)
        if i:
            v = pltpu.roll(v, cz - i, 1)
        for step in (1, 2, 4):
            v = v + pltpu.roll(v, step, 1)
        sp[i] = v

    def tall(v):
        return jnp.concatenate(
            [jnp.broadcast_to(v[j:j + 1], (COARSEN, cz)) for j in range(rows)], axis=0)

    sums = []
    for i in range(ions):
        v = sp[i]
        lift = tall(v[:rows])
        lo, hi = tall(v[rows:2 * rows]), tall(v[2 * rows:3 * rows])
        base = yz_sum(lift) + lift
        base += jnp.where(first_y, v[3 * rows:3 * rows + 1], 0.0)
        base += jnp.where(last_y, v[3 * rows + 1:3 * rows + 2], 0.0)
        numer = jnp.zeros((cy, cz), F32)
        denom = jnp.zeros((cy, cz), F32)
        for h in range(2):
            for k in range(kp):
                side = lift
                low_side = p if h else jnp.logical_not(p)
                high_side = jnp.logical_not(p) if h else p
                if k == 0:
                    side = jnp.where(low_side, lo, side)
                if k == kp - 1:
                    side = jnp.where(high_side, hi, side)
                im = diag[h, i, k] * lift - spread_ref[i] * condp[h, k] * (base + side)
                image[h, i, k] = im
                numer += rhs[h, i, k] * im
                denom += im * im
        sums.append((jnp.sum(numer, axis=0, keepdims=True), jnp.sum(denom, axis=0, keepdims=True)))
    part[me] = jnp.concatenate([n for n, _ in sums] + [m for _, m in sums], axis=0)
    spread_out(part, psend, precv)
    all_of(part, precv)
    whole = jnp.sum(jnp.sum(part[...], axis=0), axis=1, keepdims=True)
    weight = whole[:ions] / (whole[ions:] + EPSILON)
    wv[...] = jnp.broadcast_to(weight, (ions, cz))

    for i in range(ions):
        wt = wv[i:i + 1]
        lifted = wt * tall(sp[i, :rows])
        for k in range(kp):
            red, black = d[0, i, k], d[1, i, k]
            up_ref[i, 2 * k] = state_ref[i, 2 * k] + (jnp.where(p, black, red) + lifted)
            up_ref[i, 2 * k + 1] = state_ref[i, 2 * k + 1] + (jnp.where(p, red, black) + lifted)
            red = rhs[0, i, k] - wt * image[0, i, k]
            black = rhs[1, i, k] - wt * image[1, i, k]
            res_ref[i, 2 * k] = jnp.where(p, black, red)
            res_ref[i, 2 * k + 1] = jnp.where(p, red, black)

    for e in range(3):
        for k in range(4):
            @pl.when(has[k])
            def _():
                copy(e, k).wait_send()
    all_of(gath, gsend)
    all_of(part, psend)


def on_device(n_span, n_width, state, source, conductance, rebar_cover, colour, diffusivity, binding):
    ions, cx, cy, cz = state.shape
    kp = cx // 2
    total = n_span * n_width
    rows = cy // COARSEN
    half = pltpu.VMEM((2, ions, kp, cy, cz), F32)
    pair = pltpu.VMEM((2, kp, cy, cz), F32)
    vmem = pl.BlockSpec(memory_space=pltpu.VMEM)
    smem = pl.BlockSpec(memory_space=pltpu.SMEM)
    dma = pltpu.SemaphoreType.DMA
    return pl.pallas_call(
        functools.partial(kernel, n_span, n_width, ions, cx, cy, cz),
        out_shape=(jax.ShapeDtypeStruct(state.shape, F32),) * 2,
        in_specs=[vmem] * 4 + [smem] * 3,
        out_specs=(vmem, vmem),
        scratch_shapes=[
            pltpu.VMEM((2, 2, ions, cy, cz), F32),
            pltpu.VMEM((3, 2, ions, cy, cz), F32),
            pltpu.VMEM((3, 2, ions, 2 * kp, cz), F32),
            pltpu.VMEM((3, 2, ions, 2 * kp, cz), F32),
            pltpu.VMEM((total, 2 * rows, cz), F32),
            pltpu.VMEM((total, 2 * ions, cz), F32),
            pair, pair, half, half, half, half, half, half,
            pltpu.VMEM((ions, cy, cz), F32),
            pltpu.VMEM((ions, cy, cz), F32),
            pltpu.VMEM((cy, cz), F32),
            pltpu.VMEM((n_span, n_width * rows, cz), F32),
            pltpu.VMEM((n_span, n_width * rows, cz), F32),
            pltpu.VMEM((n_span + 2, n_width * rows, cz), F32),
            pltpu.VMEM((ions, 16, cz), F32),
            pltpu.VMEM((ions, cz), F32),
            dma((3, 4)), dma((3, 4)), dma, dma, dma, dma,
        ],
        compiler_params=pltpu.CompilerParams(
            collective_id=0, has_side_effects=True, vmem_limit_bytes=40 * 1024 * 1024
        ),
    )(state, source, conductance, rebar_cover, colour, diffusivity, binding)


def solution(mesh):
    in_specs = (
        P(None, "span", "width", None),
        P(None, "span", "width", None),
        P("span", "width", None),
        P("span", "width", None),
        P("span", "width"),
        P(),
        P(),
    )
    out_specs = (P(None, "span", "width", None), P(None, "span", "width", None))
    return jax.shard_map(
        functools.partial(on_device, mesh.shape["span"], mesh.shape["width"]),
        mesh=mesh, in_specs=in_specs, out_specs=out_specs, check_vma=False,
    )
```

time: 472 us -> 47.5 us (0.10)
  starting transfers between devices: 208 us -> 0 us
  waiting for transfers between devices: 147 us -> 0 us
  local copies, waits for them, and re-layouts: 53 us -> 5.48 us
  Pallas kernels: 0 us -> 40.4 us
  blocking collectives: 38.1 us -> 0 us
  other arithmetic: 19.2 us -> 0 us
    ppermute x100 -> x0, starting transfers between devices: 208 us -> none  [the longest x50 143 us: padded(): before = lax.ppermute(last, axis, up)]
    ppermute x100 -> x0, waiting for transfers between devices: 147 us -> none  [the longest x50 132 us: padded(): after = lax.ppermute(first, axis, down)]
    pallas_call x0 -> x1, Pallas kernels: none -> 40.4 us  [on_device(): pl.pallas_call(functools.partial(kernel, n_span, n_width, ions, cx, cy, c...]
    psum x1 -> x0, blocking collectives: 38.1 us -> none  [on_device(): lax.psum((jnp.sum(fine * image, axis=(1, 2, 3)), jnp.sum(image * image, a...]
    scatter x9 -> x0, local copies, waits for them, and re-layouts: 26.2 us -> none  [on_device(): full = frozen.at[:, 1:-1, 1:-1, :].set(delta)]
    unnamed x50 -> x14, local copies, waits for them, and re-layouts: 15.6 us -> 5.48 us
    slice x48 -> x0, local copies, waits for them, and re-layouts: 9.26 us -> none  [the longest x41 7.5 us: later_z(): return jnp.pad(value[..., 1:], ((0, 0), (0, 0), (0, 0), (0, 1)))]
    select_n x16 -> x0, other arithmetic: 9.12 us -> none  [on_device(): delta = jnp.where(chosen, fresh, delta)]
  transfers between devices with their start and end apart: 100 -> 0, of which waited for: 53 -> 0; matrix products, arithmetic and copies ran while one was open for 1% -> 0% of each run, Pallas kernels for 0% -> 0%
where the time goes in v1:
time: 47.5 us; the launch traced here: 47.3 us
  Pallas kernels  40.4 us (85%)
  local copies, waits for them, and re-layouts  5.48 us (12%)
  between operations  1.35 us (3%)
    pallas_call x1, Pallas kernels, on_device(): pl.pallas_call(functools.partial(kernel, n_span, n_width, ions, cx, cy, c...  40.4 us
    unnamed x14, local copies, waits for them, and re-layouts  5.48 us

profile of v1, /device:TPU:0, one launch (start us, length us, event | category | flops | bytes accessed | tf_op | source)
XLA Modules:
  0.0 47.3 jit_solution(210290081219843551)
XLA Ops:
  0.6 0.0 copy-start.5
  0.6 0.0 copy-start.4
  1.3 0.0 copy-done.5
  1.3 0.0 copy-done.4
  1.3 0.0 copy-start
  1.3 1.0 %copy-done = f32[4,8,32,128]{3,2,1,0:T(8,128)S(1)} copy-done((f32[4,8,32,128]{3,2,1,0:T(8,128)S(1)}, f32[4,8,32,128]{3,2,1,0:T(8,128)}, u32[]{:S(2)}) %copy-start) | copy-done | bytes 524312
  2.4 0.0 copy-start.1
  2.4 1.0 %copy-done.1 = f32[4,8,32,128]{3,2,1,0:T(8,128)S(1)} copy-done((f32[4,8,32,128]{3,2,1,0:T(8,128)S(1)}, f32[4,8,32,128]{3,2,1,0:T(8,128)}, u32[]{:S(2)}) %copy-start.1) | copy-done | bytes 524312
  3.4 0.0 copy-start.2
  3.4 0.9 %copy-done.2 = f32[8,32,128]{2,1,0:T(8,128)S(1)} copy-done((f32[8,32,128]{2,1,0:T(8,128)S(1)}, f32[8,32,128]{2,1,0:T(8,128)}, u32[]{:S(2)}) %copy-start.2) | copy-done | bytes 131096
  4.3 0.0 copy-start.3
  4.3 0.9 %copy-done.3 = s32[8,32,128]{2,1,0:T(8,128)S(1)} copy-done((s32[8,32,128]{2,1,0:T(8,128)S(1)}, s32[8,32,128]{2,1,0:T(8,128)}, u32[]{:S(2)}) %copy-start.3) | copy-done | bytes 131096
  5.2 40.4 %shard_map.86 = (f32[4,8,32,128]{3,2,1,0:T(8,128)S(1)}, f32[4,8,32,128]{3,2,1,0:T(8,128)S(1)}) custom-call(f32[4,8,32,128]{3,2,1,0:T(8,128)S(1)} %copy-done, f32[4,8,32,128]{3,2,1,0:T(8,128)S(1)} %copy-done.1, f32[8,32,128]{2,1,0:T(8,128)S(1)} %copy-done.2, s32[8,32,128]{2,1,0:T(8,128)S(1)} %copy-done.3, s32[1,1]{1,0:T(1,128)S(6)} %copy.11.colour_ref, ...), custom_call_target="tpu_custom_call" | custom-call | tf_op jit(solution)/shard_map/pallas_call | solution.py:378
  45.7 0.8 %copy.12 = f32[4,8,32,128]{3,2,1,0:T(8,128)} copy(f32[4,8,32,128]{3,2,1,0:T(8,128)S(1)} %get-tuple-element.4) | data formatting | bytes 1048576
  46.5 0.8 %copy.13 = f32[4,8,32,128]{3,2,1,0:T(8,128)} copy(f32[4,8,32,128]{3,2,1,0:T(8,128)S(1)} %get-tuple-element.5) | data formatting | bytes 1048576
Async XLA Ops:
  0.6 0.7 %copy-start.5 = (f32[4]{0:T(128)S(1)}, f32[4]{0:T(128)}, u32[]{:S(2)}) copy-start(f32[4]{0:T(128)} %strength_ref.1) | copy-start | bytes 52
  0.6 0.7 %copy-start.4 = (f32[4]{0:T(128)S(1)}, f32[4]{0:T(128)}, u32[]{:S(2)}) copy-start(f32[4]{0:T(128)} %spread_ref.1) | copy-start | bytes 52
  1.3 1.0 %copy-start = (f32[4,8,32,128]{3,2,1,0:T(8,128)S(1)}, f32[4,8,32,128]{3,2,1,0:T(8,128)}, u32[]{:S(2)}) copy-start(f32[4,8,32,128]{3,2,1,0:T(8,128)} %state_ref.1) | copy-start | bytes 1572868
  2.4 1.0 %copy-start.1 = (f32[4,8,32,128]{3,2,1,0:T(8,128)S(1)}, f32[4,8,32,128]{3,2,1,0:T(8,128)}, u32[]{:S(2)}) copy-start(f32[4,8,32,128]{3,2,1,0:T(8,128)} %source_ref.1) | copy-start | bytes 1572868
  3.4 0.9 %copy-start.2 = (f32[8,32,128]{2,1,0:T(8,128)S(1)}, f32[8,32,128]{2,1,0:T(8,128)}, u32[]{:S(2)}) copy-start(f32[8,32,128]{2,1,0:T(8,128)} %cond_ref.1) | copy-start | bytes 393220
  4.3 0.9 %copy-start.3 = (s32[8,32,128]{2,1,0:T(8,128)S(1)}, s32[8,32,128]{2,1,0:T(8,128)}, u32[]{:S(2)}) copy-start(s32[8,32,128]{2,1,0:T(8,128)} %cover_ref.1) | copy-start | bytes 393220

commit v2 on v1

--- a/solution.py
+++ b/solution.py
@@ -18,16 +18,14 @@
 
 def kernel(
     n_span, n_width, ions, cx, cy, cz,
-    state_ref, source_ref, cond_ref, cover_ref, colour_ref, spread_ref, strength_ref,
+    state_hbm, source_hbm, cond_hbm, cover_hbm, colour_ref, spread_ref, strength_ref,
     up_ref, res_ref,
-    xs, xh, ys, yh, gath, part, condp, coverp, rhs, diag, c, a, d, image,
+    state_ref, source_ref, cond_ref, cover_ref, xs, xh, ys, yh, first, gath, second, part, condp, coverp, rhs, diag, c, a, d, image,
     mx, fx, cx_sum, aj, cj, ej, sp, wv,
-    send_sem, recv_sem, gsend, grecv, psend, precv,
+    send_sem, recv_sem, gsend, grecv, psend, precv, in_sem,
 ):
     s = lax.axis_index("span")
     w = lax.axis_index("width")
-    total_dev = n_span * n_width
-    me = s * n_width + w
     kp = cx // 2
     rows = cy // COARSEN
     row = lax.broadcasted_iota(jnp.int32, (cy, cz), 0)
@@ -36,15 +34,25 @@
     first_y, last_y = row == 0, row == cy - 1
     first_z, last_z = lane == 0, lane == cz - 1
 
+    loads = [
+        pltpu.make_async_copy(src, dst, in_sem.at[k])
+        for k, (src, dst) in enumerate((
+            (state_hbm, state_ref), (cond_hbm, cond_ref),
+            (cover_hbm, cover_ref), (source_hbm, source_ref)))
+    ]
+    for load in loads:
+        load.start()
+
     barrier = pltpu.get_barrier_semaphore()
 
-    def partner(off):
-        other = lax.rem(me + off, total_dev)
-        return (other // n_width, other % n_width)
-
-    @pl.loop(1, total_dev)
+    for off in range(1, n_width):
+        pl.semaphore_signal(
+            barrier, inc=1, device_id=(s, lax.rem(w + off, n_width)), device_id_type=MESH)
+
+    @pl.loop(1, n_span)
     def _(off):
-        pl.semaphore_signal(barrier, inc=1, device_id=partner(off), device_id_type=MESH)
+        pl.semaphore_signal(
+            barrier, inc=1, device_id=(lax.rem(s + off, n_span), w), device_id_type=MESH)
 
     def split(x):
         pairs = x.reshape(kp, 2, cy, cz)
@@ -136,10 +144,13 @@
         put_y(0, i, *split(state_ref[i]))
         return 0
 
+    loads[0].wait()
     lax.fori_loop(0, ions, pack_state, 0)
-    pl.semaphore_wait(barrier, total_dev - 1)
+    pl.semaphore_wait(barrier, n_span + n_width - 2)
     send(0, range(4))
 
+    for load in loads[1:]:
+        load.wait()
     condp[0], condp[1] = split(cond_ref[...])
     coverp[0], coverp[1] = split(cover_ref[...].astype(F32))
     cx_sum[...] = jnp.sum(cond_ref[...], axis=0)
@@ -190,7 +201,7 @@
         put_x(1, i, red, black)
         return 0
 
-    lax.fori_loop(0, ions, phase_zero, 0)
+    lax.fori_loop(0, ions, phase_zero, 0, unroll=2)
     send(1, range(4))
     receive(1)
 
@@ -206,7 +217,7 @@
         put_x(2, i, red, black)
         return 0
 
-    lax.fori_loop(0, ions, phase_one, 0)
+    lax.fori_loop(0, ions, phase_one, 0, unroll=2)
     send(2, range(4))
 
     eighth = lane % COARSEN
@@ -245,25 +256,35 @@
 
     lax.fori_loop(0, ions, fine_terms, 0)
     crhs = coarse_pack([fx[i] for i in range(ions)])
-    gath[me] = jnp.concatenate([crhs * coarse_inv, coarse_off * coarse_inv], axis=0)
-
-    def spread_out(buf, ssem, rsem):
-        @pl.loop(1, total_dev)
+    first[w] = jnp.concatenate([crhs * coarse_inv, coarse_off * coarse_inv], axis=0)
+
+    def to_row(buf, ssem, rsem):
+        for off in range(1, n_width):
+            pltpu.make_async_remote_copy(
+                src_ref=buf.at[w], dst_ref=buf.at[w], send_sem=ssem, recv_sem=rsem,
+                device_id=(s, lax.rem(w + off, n_width)), device_id_type=MESH,
+            ).start()
+
+    def to_column(buf, ssem, rsem):
+        @pl.loop(1, n_span)
         def _(off):
             pltpu.make_async_remote_copy(
-                src_ref=buf.at[me], dst_ref=buf.at[me], send_sem=ssem, recv_sem=rsem,
-                device_id=partner(off), device_id_type=MESH,
+                src_ref=buf.at[s], dst_ref=buf.at[s], send_sem=ssem, recv_sem=rsem,
+                device_id=(lax.rem(s + off, n_span), w), device_id_type=MESH,
             ).start()
 
-    def all_of(buf, sem):
-        others = buf.at[pl.ds(0, total_dev - 1)]
+    def all_of(buf, sem, count):
+        others = buf.at[pl.ds(0, count - 1)]
         pltpu.make_async_copy(others, others, sem).wait()
 
-    spread_out(gath, gsend, grecv)
-    all_of(gath, grecv)
+    to_row(first, gsend.at[0], grecv.at[0])
+    all_of(first, grecv.at[0], n_width)
+    gath[s] = first[...]
+    to_column(gath, gsend.at[1], grecv.at[1])
+    all_of(gath, grecv.at[1], n_span)
 
     wide = n_width * rows
-    g = gath[...].reshape(n_span, n_width, 2 * rows, cz)
+    g = gath[...]
     aj[...] = jnp.concatenate([g[:, k, :rows] for k in range(n_width)], axis=1)
     cj[...] = jnp.concatenate([g[:, k, rows:] for k in range(n_width)], axis=1)
     crow = lax.broadcasted_iota(jnp.int32, (wide, cz), 0)
@@ -337,9 +358,12 @@
                 numer += rhs[h, i, k] * im
                 denom += im * im
         sums.append((jnp.sum(numer, axis=0, keepdims=True), jnp.sum(denom, axis=0, keepdims=True)))
-    part[me] = jnp.concatenate([n for n, _ in sums] + [m for _, m in sums], axis=0)
-    spread_out(part, psend, precv)
-    all_of(part, precv)
+    second[w] = jnp.concatenate([n for n, _ in sums] + [m for _, m in sums], axis=0)
+    to_row(second, psend.at[0], precv.at[0])
+    all_of(second, precv.at[0], n_width)
+    part[s] = jnp.sum(second[...], axis=0)
+    to_column(part, psend.at[1], precv.at[1])
+    all_of(part, precv.at[1], n_span)
     whole = jnp.sum(jnp.sum(part[...], axis=0), axis=1, keepdims=True)
     weight = whole[:ions] / (whole[ions:] + EPSILON)
     wv[...] = jnp.broadcast_to(weight, (ions, cz))
@@ -361,14 +385,15 @@
             @pl.when(has[k])
             def _():
                 copy(e, k).wait_send()
-    all_of(gath, gsend)
-    all_of(part, psend)
+    all_of(first, gsend.at[0], n_width)
+    all_of(gath, gsend.at[1], n_span)
+    all_of(second, psend.at[0], n_width)
+    all_of(part, psend.at[1], n_span)
 
 
 def on_device(n_span, n_width, state, source, conductance, rebar_cover, colour, diffusivity, binding):
     ions, cx, cy, cz = state.shape
     kp = cx // 2
-    total = n_span * n_width
     rows = cy // COARSEN
     half = pltpu.VMEM((2, ions, kp, cy, cz), F32)
     pair = pltpu.VMEM((2, kp, cy, cz), F32)
@@ -378,15 +403,19 @@
     return pl.pallas_call(
         functools.partial(kernel, n_span, n_width, ions, cx, cy, cz),
         out_shape=(jax.ShapeDtypeStruct(state.shape, F32),) * 2,
-        in_specs=[vmem] * 4 + [smem] * 3,
+        in_specs=[pl.BlockSpec(memory_space=pltpu.HBM)] * 4 + [smem] * 3,
         out_specs=(vmem, vmem),
         scratch_shapes=[
+            pltpu.VMEM(state.shape, F32), pltpu.VMEM(state.shape, F32),
+            pltpu.VMEM(conductance.shape, F32), pltpu.VMEM(conductance.shape, jnp.int32),
             pltpu.VMEM((2, 2, ions, cy, cz), F32),
             pltpu.VMEM((3, 2, ions, cy, cz), F32),
             pltpu.VMEM((3, 2, ions, 2 * kp, cz), F32),
             pltpu.VMEM((3, 2, ions, 2 * kp, cz), F32),
-            pltpu.VMEM((total, 2 * rows, cz), F32),
-            pltpu.VMEM((total, 2 * ions, cz), F32),
+            pltpu.VMEM((n_width, 2 * rows, cz), F32),
+            pltpu.VMEM((n_span, n_width, 2 * rows, cz), F32),
+            pltpu.VMEM((n_width, 2 * ions, cz), F32),
+            pltpu.VMEM((n_span, 2 * ions, cz), F32),
             pair, pair, half, half, half, half, half, half,
             pltpu.VMEM((ions, cy, cz), F32),
             pltpu.VMEM((ions, cy, cz), F32),
@@ -396,10 +425,10 @@
             pltpu.VMEM((n_span + 2, n_width * rows, cz), F32),
             pltpu.VMEM((ions, 16, cz), F32),
             pltpu.VMEM((ions, cz), F32),
-            dma((3, 4)), dma((3, 4)), dma, dma, dma, dma,
+            dma((3, 4)), dma((3, 4)), dma((2,)), dma((2,)), dma((2,)), dma((2,)), dma((4,)),
         ],
         compiler_params=pltpu.CompilerParams(
-            collective_id=0, has_side_effects=True, vmem_limit_bytes=40 * 1024 * 1024
+            collective_id=0, has_side_effects=True, vmem_limit_bytes=60 * 1024 * 1024
         ),
     )(state, source, conductance, rebar_cover, colour, diffusivity, binding)
 

time: 47.5 us -> 43.7 us (0.920)
  local copies, waits for them, and re-layouts: 5.48 us -> 2.72 us
  Pallas kernels: 40.4 us -> 39.5 us
    unnamed x14 -> x4, local copies, waits for them, and re-layouts: 5.48 us -> 2.72 us
    pallas_call x1, Pallas kernels: 40.4 us -> 39.5 us  [on_device(): pl.pallas_call(functools.partial(kernel, n_span, n_width, ions, cx, cy, c...]
where the time goes in v2:
time: 43.7 us; the launch traced here: 43.6 us
  Pallas kernels  39.5 us (90%)
  local copies, waits for them, and re-layouts  2.72 us (6%)
  between operations  1.29 us (3%)
    pallas_call x1, Pallas kernels, on_device(): pl.pallas_call(functools.partial(kernel, n_span, n_width, ions, cx, cy, c...  39.5 us
    unnamed x4, local copies, waits for them, and re-layouts  2.72 us

profile of v2, /device:TPU:0, one launch (start us, length us, event | category | flops | bytes accessed | tf_op | source)
XLA Modules:
  0.0 43.6 jit_solution(8082549464856871065)
XLA Ops:
  1.3 39.5 %shard_map.86 = (f32[4,8,32,128]{3,2,1,0:T(8,128)}, f32[4,8,32,128]{3,2,1,0:T(8,128)}) custom-call(f32[4,8,32,128]{3,2,1,0:T(8,128)} %state_hbm.1, f32[4,8,32,128]{3,2,1,0:T(8,128)} %source_hbm.1, f32[8,32,128]{2,1,0:T(8,128)} %cond_hbm.1, s32[8,32,128]{2,1,0:T(8,128)} %cover_hbm.1, s32[1,1]{1,0:T(1,128)S(6)} %copy.11.colour_ref, f32[4]{0:T(128)} %spread_ref.1, ...), custom_call_target="tpu_custom_call" | custom-call | tf_op jit(solution)/shard_map/pallas_call | solution.py:403
  40.8 0.0 copy-start
  40.8 1.9 %copy.12 = f32[4,8,32,128]{3,2,1,0:T(8,128)} copy(f32[4,8,32,128]{3,2,1,0:T(8,128)} %get-tuple-element.4) | data formatting | bytes 1048576
  42.8 0.0 copy-done
  42.8 0.8 %copy.13 = f32[4,8,32,128]{3,2,1,0:T(8,128)} copy(f32[4,8,32,128]{3,2,1,0:T(8,128)S(1)} %copy-done) | data formatting | bytes 1048576
Async XLA Ops:
  40.8 1.9 %copy-start = (f32[4,8,32,128]{3,2,1,0:T(8,128)S(1)}, f32[4,8,32,128]{3,2,1,0:T(8,128)}, u32[]{:S(2)}) copy-start(f32[4,8,32,128]{3,2,1,0:T(8,128)} %get-tuple-element.5) | copy-start | bytes 1572868

commit v3 on v2

--- a/solution.py
+++ b/solution.py
@@ -22,7 +22,7 @@
     up_ref, res_ref,
     state_ref, source_ref, cond_ref, cover_ref, xs, xh, ys, yh, first, gath, second, part, condp, coverp, rhs, diag, c, a, d, image,
     mx, fx, cx_sum, aj, cj, ej, sp, wv,
-    send_sem, recv_sem, gsend, grecv, psend, precv, in_sem,
+    send_sem, recv_sem, gsend, grecv, psend, precv, in_sem, met,
 ):
     s = lax.axis_index("span")
     w = lax.axis_index("width")
@@ -45,14 +45,35 @@
 
     barrier = pltpu.get_barrier_semaphore()
 
-    for off in range(1, n_width):
-        pl.semaphore_signal(
-            barrier, inc=1, device_id=(s, lax.rem(w + off, n_width)), device_id_type=MESH)
-
-    @pl.loop(1, n_span)
-    def _(off):
-        pl.semaphore_signal(
-            barrier, inc=1, device_id=(lax.rem(s + off, n_span), w), device_id_type=MESH)
+    has = (s < n_span - 1, s > 0, w < n_width - 1, w > 0)
+    gets = (s > 0, s < n_span - 1, w > 0, w < n_width - 1)
+    to = ((s + 1, w), (s - 1, w), (s, w + 1), (s, w - 1))
+
+    def flip(v, bit):
+        return v + bit - 2 * bit * (v // bit % 2)
+
+    bits = [1 << k for k in range((max(n_span, n_width) - 1).bit_length())]
+    hops = [(s, flip(w, b)) for b in bits if b < n_width]
+    hops += [(flip(s, b), w) for b in bits if b < n_span]
+    far = [(s, flip(w, b)) for b in bits if 1 < b < n_width]
+    far += [(flip(s, b), w) for b in bits if 1 < b < n_span]
+    for k in range(4):
+        @pl.when(has[k])
+        def _():
+            pl.semaphore_signal(barrier, inc=1, device_id=to[k], device_id_type=MESH)
+    for other in far:
+        pl.semaphore_signal(barrier, inc=1, device_id=other, device_id_type=MESH)
+
+    def meet(which):
+        for k in which:
+            if 0 <= k < len(hops):
+                pl.semaphore_signal(
+                    met.at[k], inc=1, device_id=hops[k], device_id_type=MESH)
+
+    def met_by(which):
+        for k in which:
+            if 0 <= k < len(hops):
+                pl.semaphore_wait(met.at[k], 1)
 
     def split(x):
         pairs = x.reshape(kp, 2, cy, cz)
@@ -100,10 +121,6 @@
     def put_x(e, i, red, black):
         xs[e - 1, 0, i] = jnp.where(p, red[kp - 1], black[kp - 1])
         xs[e - 1, 1, i] = jnp.where(p, black[0], red[0])
-
-    has = (s < n_span - 1, s > 0, w < n_width - 1, w > 0)
-    gets = (s > 0, s < n_span - 1, w > 0, w < n_width - 1)
-    to = ((s + 1, w), (s - 1, w), (s, w + 1), (s, w - 1))
 
     def copy(e, k):
         if k >= 2:
@@ -146,8 +163,10 @@
 
     loads[0].wait()
     lax.fori_loop(0, ions, pack_state, 0)
-    pl.semaphore_wait(barrier, n_span + n_width - 2)
+    near = sum(g.astype(jnp.int32) for g in gets)
+    pl.semaphore_wait(barrier, near + len(far))
     send(0, range(4))
+    meet((0,))
 
     for load in loads[1:]:
         load.wait()
@@ -176,6 +195,8 @@
 
     lax.fori_loop(0, ions, local_terms, 0)
     receive(0)
+    met_by((0,))
+    meet((1,))
 
     mine = colour_ref[0, 0].astype(F32)
 
@@ -203,7 +224,11 @@
 
     lax.fori_loop(0, ions, phase_zero, 0, unroll=2)
     send(1, range(4))
+    met_by((1,))
+    meet((2,))
     receive(1)
+    met_by((2,))
+    meet((3,))
 
     def phase_one(i, _):
         near = rim(1, i)
@@ -219,6 +244,8 @@
 
     lax.fori_loop(0, ions, phase_one, 0, unroll=2)
     send(2, range(4))
+    met_by((3,))
+    meet((4,))
 
     eighth = lane % COARSEN
 
@@ -254,7 +281,11 @@
         fx[i] = total
         return 0
 
-    lax.fori_loop(0, ions, fine_terms, 0)
+    met_by((4,))
+    for k in range(5, len(hops)):
+        meet((k,))
+        met_by((k,))
+    lax.fori_loop(0, ions, fine_terms, 0, unroll=2)
     crhs = coarse_pack([fx[i] for i in range(ions)])
     first[w] = jnp.concatenate([crhs * coarse_inv, coarse_off * coarse_inv], axis=0)
 
@@ -425,7 +456,7 @@
             pltpu.VMEM((n_span + 2, n_width * rows, cz), F32),
             pltpu.VMEM((ions, 16, cz), F32),
             pltpu.VMEM((ions, cz), F32),
-            dma((3, 4)), dma((3, 4)), dma((2,)), dma((2,)), dma((2,)), dma((2,)), dma((4,)),
+            dma((3, 4)), dma((3, 4)), dma((2,)), dma((2,)), dma((2,)), dma((2,)), dma((4,)), pltpu.SemaphoreType.REGULAR((max(5, (n_span - 1).bit_length() + (n_width - 1).bit_length()),)),
         ],
         compiler_params=pltpu.CompilerParams(
             collective_id=0, has_side_effects=True, vmem_limit_bytes=60 * 1024 * 1024

time: 43.7 us -> 43 us (0.984)
  Pallas kernels: 39.5 us -> 38.8 us
    pallas_call x1, Pallas kernels: 39.5 us -> 38.8 us  [on_device(): pl.pallas_call(functools.partial(kernel, n_span, n_width, ions, cx, cy, c...]
where the time goes in v3:
time: 43 us; the launch traced here: 42.9 us
  Pallas kernels  38.8 us (90%)
  local copies, waits for them, and re-layouts  2.72 us (6%)
  between operations  1.29 us (3%)
    pallas_call x1, Pallas kernels, on_device(): pl.pallas_call(functools.partial(kernel, n_span, n_width, ions, cx, cy, c...  38.8 us
    unnamed x4, local copies, waits for them, and re-layouts  2.72 us

profile of v3, /device:TPU:0, one launch (start us, length us, event | category | flops | bytes accessed | tf_op | source)
XLA Modules:
  0.0 42.9 jit_solution(2208339520763207169)
XLA Ops:
  1.3 38.8 %shard_map.86 = (f32[4,8,32,128]{3,2,1,0:T(8,128)}, f32[4,8,32,128]{3,2,1,0:T(8,128)}) custom-call(f32[4,8,32,128]{3,2,1,0:T(8,128)} %state_hbm.1, f32[4,8,32,128]{3,2,1,0:T(8,128)} %source_hbm.1, f32[8,32,128]{2,1,0:T(8,128)} %cond_hbm.1, s32[8,32,128]{2,1,0:T(8,128)} %cover_hbm.1, s32[1,1]{1,0:T(1,128)S(6)} %copy.11.colour_ref, f32[4]{0:T(128)} %spread_ref.1, ...), custom_call_target="tpu_custom_call" | custom-call | tf_op jit(solution)/shard_map/pallas_call | solution.py:434
  40.1 0.0 copy-start
  40.1 1.9 %copy.12 = f32[4,8,32,128]{3,2,1,0:T(8,128)} copy(f32[4,8,32,128]{3,2,1,0:T(8,128)} %get-tuple-element.4) | data formatting | bytes 1048576
  42.1 0.0 copy-done
  42.1 0.8 %copy.13 = f32[4,8,32,128]{3,2,1,0:T(8,128)} copy(f32[4,8,32,128]{3,2,1,0:T(8,128)S(1)} %copy-done) | data formatting | bytes 1048576
Async XLA Ops:
  40.1 1.9 %copy-start = (f32[4,8,32,128]{3,2,1,0:T(8,128)S(1)}, f32[4,8,32,128]{3,2,1,0:T(8,128)}, u32[]{:S(2)}) copy-start(f32[4,8,32,128]{3,2,1,0:T(8,128)} %get-tuple-element.5) | copy-start | bytes 1572868

commit v4 on v3

--- a/solution.py
+++ b/solution.py
@@ -122,31 +122,34 @@
         xs[e - 1, 0, i] = jnp.where(p, red[kp - 1], black[kp - 1])
         xs[e - 1, 1, i] = jnp.where(p, black[0], red[0])
 
-    def copy(e, k):
+    pair_of = ions // 2
+
+    def copy(e, k, g):
+        own = pl.ds(g * pair_of, pair_of)
         if k >= 2:
-            src, dst = ys.at[e, k - 2], yh.at[e, k - 2]
+            src, dst = ys.at[e, k - 2, own], yh.at[e, k - 2, own]
         else:
-            dst = xh.at[e, k]
+            dst = xh.at[e, k, own]
             if e == 0:
-                src = state_ref.at[:, cx - 1] if k == 0 else state_ref.at[:, 0]
+                src = state_ref.at[own, cx - 1] if k == 0 else state_ref.at[own, 0]
             else:
-                src = xs.at[e - 1, k]
+                src = xs.at[e - 1, k, own]
         return pltpu.make_async_remote_copy(
-            src_ref=src, dst_ref=dst, send_sem=send_sem.at[e, k], recv_sem=recv_sem.at[e, k],
+            src_ref=src, dst_ref=dst, send_sem=send_sem.at[e, k, g], recv_sem=recv_sem.at[e, k, g],
             device_id=to[k], device_id_type=MESH,
         )
 
-    def send(e, which):
-        for k in which:
+    def send(e, g):
+        for k in range(4):
             @pl.when(has[k])
             def _():
-                copy(e, k).start()
-
-    def receive(e):
+                copy(e, k, g).start()
+
+    def receive(e, g):
         for k in range(4):
             @pl.when(gets[k])
             def _():
-                copy(e, k).wait_recv()
+                copy(e, k, g).wait_recv()
 
     for k in range(4):
         @pl.when(jnp.logical_not(gets[k]))
@@ -165,7 +168,8 @@
     lax.fori_loop(0, ions, pack_state, 0)
     near = sum(g.astype(jnp.int32) for g in gets)
     pl.semaphore_wait(barrier, near + len(far))
-    send(0, range(4))
+    send(0, 0)
+    send(0, 1)
     meet((0,))
 
     for load in loads[1:]:
@@ -194,7 +198,6 @@
         return 0
 
     lax.fori_loop(0, ions, local_terms, 0)
-    receive(0)
     met_by((0,))
     meet((1,))
 
@@ -222,11 +225,16 @@
         put_x(1, i, red, black)
         return 0
 
-    lax.fori_loop(0, ions, phase_zero, 0, unroll=2)
-    send(1, range(4))
+    def halves(e, body):
+        for g in range(2):
+            receive(e, g)
+            lax.fori_loop(g * pair_of, (g + 1) * pair_of, body, 0, unroll=2)
+            if e < 2:
+                send(e + 1, g)
+
+    halves(0, phase_zero)
     met_by((1,))
     meet((2,))
-    receive(1)
     met_by((2,))
     meet((3,))
 
@@ -242,8 +250,7 @@
         put_x(2, i, red, black)
         return 0
 
-    lax.fori_loop(0, ions, phase_one, 0, unroll=2)
-    send(2, range(4))
+    halves(1, phase_one)
     met_by((3,))
     meet((4,))
 
@@ -267,7 +274,6 @@
     coarse_diag = coarse_pack([mx[i] for i in range(ions)]) + 6.0 * coarse_off
     coarse_inv = 1.0 / jnp.where(eighth[:rows] < ions, coarse_diag, 1.0)
 
-    receive(2)
 
     def fine_terms(i, _):
         near = rim(2, i)
@@ -285,7 +291,7 @@
     for k in range(5, len(hops)):
         meet((k,))
         met_by((k,))
-    lax.fori_loop(0, ions, fine_terms, 0, unroll=2)
+    halves(2, fine_terms)
     crhs = coarse_pack([fx[i] for i in range(ions)])
     first[w] = jnp.concatenate([crhs * coarse_inv, coarse_off * coarse_inv], axis=0)
 
@@ -415,7 +421,8 @@
         for k in range(4):
             @pl.when(has[k])
             def _():
-                copy(e, k).wait_send()
+                copy(e, k, 0).wait_send()
+                copy(e, k, 1).wait_send()
     all_of(first, gsend.at[0], n_width)
     all_of(gath, gsend.at[1], n_span)
     all_of(second, psend.at[0], n_width)
@@ -456,7 +463,7 @@
             pltpu.VMEM((n_span + 2, n_width * rows, cz), F32),
             pltpu.VMEM((ions, 16, cz), F32),
             pltpu.VMEM((ions, cz), F32),
-            dma((3, 4)), dma((3, 4)), dma((2,)), dma((2,)), dma((2,)), dma((2,)), dma((4,)), pltpu.SemaphoreType.REGULAR((max(5, (n_span - 1).bit_length() + (n_width - 1).bit_length()),)),
+            dma((3, 4, 2)), dma((3, 4, 2)), dma((2,)), dma((2,)), dma((2,)), dma((2,)), dma((4,)), pltpu.SemaphoreType.REGULAR((max(5, (n_span - 1).bit_length() + (n_width - 1).bit_length()),)),
         ],
         compiler_params=pltpu.CompilerParams(
             collective_id=0, has_side_effects=True, vmem_limit_bytes=60 * 1024 * 1024

time: 43 us -> 40.4 us (0.940)
  Pallas kernels: 38.8 us -> 36.2 us
    pallas_call x1, Pallas kernels: 38.8 us -> 36.2 us  [on_device(): pl.pallas_call(functools.partial(kernel, n_span, n_width, ions, cx, cy, c...]
where the time goes in v4:
time: 40.4 us; the launch traced here: 40.2 us
  Pallas kernels  36.2 us (90%)
  local copies, waits for them, and re-layouts  2.72 us (7%)
  between operations  1.29 us (3%)
    pallas_call x1, Pallas kernels, on_device(): pl.pallas_call(functools.partial(kernel, n_span, n_width, ions, cx, cy, c...  36.2 us
    unnamed x4, local copies, waits for them, and re-layouts  2.72 us

profile of v4, /device:TPU:0, one launch (start us, length us, event | category | flops | bytes accessed | tf_op | source)
XLA Modules:
  0.0 40.2 jit_solution(17322575656610933402)
XLA Ops:
  1.3 36.2 %shard_map.86 = (f32[4,8,32,128]{3,2,1,0:T(8,128)}, f32[4,8,32,128]{3,2,1,0:T(8,128)}) custom-call(f32[4,8,32,128]{3,2,1,0:T(8,128)} %state_hbm.1, f32[4,8,32,128]{3,2,1,0:T(8,128)} %source_hbm.1, f32[8,32,128]{2,1,0:T(8,128)} %cond_hbm.1, s32[8,32,128]{2,1,0:T(8,128)} %cover_hbm.1, s32[1,1]{1,0:T(1,128)S(6)} %copy.11.colour_ref, f32[4]{0:T(128)} %spread_ref.1, ...), custom_call_target="tpu_custom_call" | custom-call | tf_op jit(solution)/shard_map/pallas_call | solution.py:441
  37.5 0.0 copy-start
  37.5 1.9 %copy.12 = f32[4,8,32,128]{3,2,1,0:T(8,128)} copy(f32[4,8,32,128]{3,2,1,0:T(8,128)} %get-tuple-element.4) | data formatting | bytes 1048576
  39.4 0.0 copy-done
  39.4 0.8 %copy.13 = f32[4,8,32,128]{3,2,1,0:T(8,128)} copy(f32[4,8,32,128]{3,2,1,0:T(8,128)S(1)} %copy-done) | data formatting | bytes 1048576
Async XLA Ops:
  37.5 1.9 %copy-start = (f32[4,8,32,128]{3,2,1,0:T(8,128)S(1)}, f32[4,8,32,128]{3,2,1,0:T(8,128)}, u32[]{:S(2)}) copy-start(f32[4,8,32,128]{3,2,1,0:T(8,128)} %get-tuple-element.5) | copy-start | bytes 1572868

commit v5 on v4

--- a/solution.py
+++ b/solution.py
@@ -20,7 +20,7 @@
     n_span, n_width, ions, cx, cy, cz,
     state_hbm, source_hbm, cond_hbm, cover_hbm, colour_ref, spread_ref, strength_ref,
     up_ref, res_ref,
-    state_ref, source_ref, cond_ref, cover_ref, xs, xh, ys, yh, first, gath, second, part, condp, coverp, rhs, diag, c, a, d, image,
+    state_ref, source_ref, cond_ref, cover_ref, xs, xh, ys, yh, first, gath, part, condp, coverp, rhs, diag, c, a, d, image,
     mx, fx, cx_sum, aj, cj, ej, sp, wv,
     send_sem, recv_sem, gsend, grecv, psend, precv, in_sem, met,
 ):
@@ -395,12 +395,19 @@
                 numer += rhs[h, i, k] * im
                 denom += im * im
         sums.append((jnp.sum(numer, axis=0, keepdims=True), jnp.sum(denom, axis=0, keepdims=True)))
-    second[w] = jnp.concatenate([n for n, _ in sums] + [m for _, m in sums], axis=0)
-    to_row(second, psend.at[0], precv.at[0])
-    all_of(second, precv.at[0], n_width)
-    part[s] = jnp.sum(second[...], axis=0)
-    to_column(part, psend.at[1], precv.at[1])
-    all_of(part, precv.at[1], n_span)
+    me = s * n_width + w
+    part[me] = jnp.concatenate([n for n, _ in sums] + [m for _, m in sums], axis=0)
+    everyone = n_span * n_width
+
+    @pl.loop(1, everyone)
+    def _(off):
+        other = lax.rem(me + off, everyone)
+        pltpu.make_async_remote_copy(
+            src_ref=part.at[me], dst_ref=part.at[me], send_sem=psend, recv_sem=precv,
+            device_id=(other // n_width, other % n_width), device_id_type=MESH,
+        ).start()
+
+    all_of(part, precv, everyone)
     whole = jnp.sum(jnp.sum(part[...], axis=0), axis=1, keepdims=True)
     weight = whole[:ions] / (whole[ions:] + EPSILON)
     wv[...] = jnp.broadcast_to(weight, (ions, cz))
@@ -425,8 +432,7 @@
                 copy(e, k, 1).wait_send()
     all_of(first, gsend.at[0], n_width)
     all_of(gath, gsend.at[1], n_span)
-    all_of(second, psend.at[0], n_width)
-    all_of(part, psend.at[1], n_span)
+    all_of(part, psend, everyone)
 
 
 def on_device(n_span, n_width, state, source, conductance, rebar_cover, colour, diffusivity, binding):
@@ -452,8 +458,7 @@
             pltpu.VMEM((3, 2, ions, 2 * kp, cz), F32),
             pltpu.VMEM((n_width, 2 * rows, cz), F32),
             pltpu.VMEM((n_span, n_width, 2 * rows, cz), F32),
-            pltpu.VMEM((n_width, 2 * ions, cz), F32),
-            pltpu.VMEM((n_span, 2 * ions, cz), F32),
+            pltpu.VMEM((n_span * n_width, 2 * ions, cz), F32),
             pair, pair, half, half, half, half, half, half,
             pltpu.VMEM((ions, cy, cz), F32),
             pltpu.VMEM((ions, cy, cz), F32),
@@ -463,7 +468,7 @@
             pltpu.VMEM((n_span + 2, n_width * rows, cz), F32),
             pltpu.VMEM((ions, 16, cz), F32),
             pltpu.VMEM((ions, cz), F32),
-            dma((3, 4, 2)), dma((3, 4, 2)), dma((2,)), dma((2,)), dma((2,)), dma((2,)), dma((4,)), pltpu.SemaphoreType.REGULAR((max(5, (n_span - 1).bit_length() + (n_width - 1).bit_length()),)),
+            dma((3, 4, 2)), dma((3, 4, 2)), dma((2,)), dma((2,)), dma, dma, dma((4,)), pltpu.SemaphoreType.REGULAR((max(5, (n_span - 1).bit_length() + (n_width - 1).bit_length()),)),
         ],
         compiler_params=pltpu.CompilerParams(
             collective_id=0, has_side_effects=True, vmem_limit_bytes=60 * 1024 * 1024

time: 40.4 us -> 39.7 us (0.983)
  Pallas kernels: 36.2 us -> 35.5 us
    pallas_call x1, Pallas kernels: 36.2 us -> 35.5 us  [on_device(): pl.pallas_call(functools.partial(kernel, n_span, n_width, ions, cx, cy, c...]
where the time goes in v5:
time: 39.7 us; the launch traced here: 39.5 us
  Pallas kernels  35.5 us (89%)
  local copies, waits for them, and re-layouts  2.72 us (7%)
  between operations  1.29 us (3%)
    pallas_call x1, Pallas kernels, on_device(): pl.pallas_call(functools.partial(kernel, n_span, n_width, ions, cx, cy, c...  35.5 us
    unnamed x4, local copies, waits for them, and re-layouts  2.72 us

profile of v5, /device:TPU:0, one launch (start us, length us, event | category | flops | bytes accessed | tf_op | source)
XLA Modules:
  0.0 39.5 jit_solution(11173694350150328114)
XLA Ops:
  1.3 35.5 %shard_map.86 = (f32[4,8,32,128]{3,2,1,0:T(8,128)}, f32[4,8,32,128]{3,2,1,0:T(8,128)}) custom-call(f32[4,8,32,128]{3,2,1,0:T(8,128)} %state_hbm.1, f32[4,8,32,128]{3,2,1,0:T(8,128)} %source_hbm.1, f32[8,32,128]{2,1,0:T(8,128)} %cond_hbm.1, s32[8,32,128]{2,1,0:T(8,128)} %cover_hbm.1, s32[1,1]{1,0:T(1,128)S(6)} %copy.11.colour_ref, f32[4]{0:T(128)} %spread_ref.1, ...), custom_call_target="tpu_custom_call" | custom-call | tf_op jit(solution)/shard_map/pallas_call | solution.py:447
  36.8 0.0 copy-start
  36.8 1.9 %copy.12 = f32[4,8,32,128]{3,2,1,0:T(8,128)} copy(f32[4,8,32,128]{3,2,1,0:T(8,128)} %get-tuple-element.4) | data formatting | bytes 1048576
  38.7 0.0 copy-done
  38.7 0.8 %copy.13 = f32[4,8,32,128]{3,2,1,0:T(8,128)} copy(f32[4,8,32,128]{3,2,1,0:T(8,128)S(1)} %copy-done) | data formatting | bytes 1048576
Async XLA Ops:
  36.8 1.9 %copy-start = (f32[4,8,32,128]{3,2,1,0:T(8,128)S(1)}, f32[4,8,32,128]{3,2,1,0:T(8,128)}, u32[]{:S(2)}) copy-start(f32[4,8,32,128]{3,2,1,0:T(8,128)} %get-tuple-element.5) | copy-start | bytes 1572868
